TPU v7x, 1024 devices: a whole 4x4x32 slice. The times are simulated.
1024 devices in a mesh: lat: 64 (over z, core), lon: 16 (over x, y).
Axes of the slice: x: 4, y: 4, z: 32, core: 2. Of those that a mesh axis runs over, the one named last changes fastest.
Arguments:
- spectral: bfloat16 [640, 2, 128, 640], P('lat', None, 'lon'), may hold values from -6 to 6
- wavenumber_of_slot: int32 [640], replicated, may hold values from 0 to 639, each once
- filter_strength: float32 [128], P('lon'), may hold values from 0.1 to 10
- courant: bfloat16 [2, 640, 1280, 128], P(None, 'lat', 'lon'), may hold values from -0.59765625 to 0.59765625
- sunlit_blocks: int32 [64, 16, 12], P('lat', 'lon'), may hold values from 0 to 49, as said below
- sunlit_owner: int32 [64, 16, 12, 1], P('lat', 'lon'), may hold values from 0 to 15; in each aligned block of 12 rows (0 to 11, 12 to 23, ..., all dimensions but the last counted through in order) at most 2 rows name the same one
- radiation_in: bfloat16 [16, 128, 512], P('lon'), may hold values from -0.5 to 0.5
- radiation_mid: bfloat16 [16, 512, 512], P('lon'), may hold values from -0.25 to 0.25
- radiation_out: bfloat16 [16, 512, 128], P('lon'), may hold values from -0.25 to 0.25
Outputs:
- advected: float32 [640, 1280, 128], P('lat', 'lon')
- heating: bfloat16 [640, 1280, 128], P('lat', 'lon')
Inputs may be any that keep to these rules, and one draw needn't show every extreme that they name: `wavenumber_of_slot`: each of 0 to 639 exactly once. `sunlit_blocks`: the 12 block numbers of one device are distinct. `sunlit_owner`: among the 12 blocks of one device no regime appears more than 2 times, and some device names some regime exactly 2 times.
All inputs are finite; a program needn't handle non-finite values.
Results may differ from a plain program's by a relative error of at most 0.015.
Values may be sent and summed in bfloat16 or wider, within the bound.
A program may use at most 32 MiB of HBM per device.

v0:
```python
import math

import jax
import jax.numpy as jnp
from jax import lax
from jax.sharding import PartitionSpec as P

NLAT = 640
NLON = 1280
BC = 16


def with_halo(array, sides, width):
    for axis, dim in sides:
        count, length = (lax.axis_size(axis), array.shape[dim])
        up = [(i, (i + 1) % count) for i in range(count)]
        down = [(j, i) for i, j in up]
        last = lax.slice_in_dim(array, length - width, length, axis=dim)
        leading = lax.slice_in_dim(array, 0, width, axis=dim)
        before = lax.ppermute(last, axis, up)
        after = lax.ppermute(leading, axis, down)
        array = jnp.concatenate([before, array, after], axis=dim)
    return array


def latitude_table(degrees, latitudes):
    degree_grid = lax.broadcasted_iota(jnp.int32, (degrees, latitudes), 0)
    row_index = lax.broadcasted_iota(jnp.int32, (degrees, latitudes), 1)
    phase_count = degree_grid * (2 * row_index + 1) % (4 * latitudes)
    phase_angle = phase_count.astype(jnp.float32) * (math.pi / (2.0 * latitudes))
    return (jnp.cos(phase_angle) * math.sqrt(2.0 / degrees)).astype(jnp.bfloat16)


def longitude_table(zonal_waves, longitudes):
    total_count = zonal_waves.shape[0]
    column_index = lax.broadcasted_iota(jnp.int32, (total_count, longitudes), 1)
    phase_count = zonal_waves[:, None] * column_index % longitudes
    phase_angle = phase_count.astype(jnp.float32) * (2.0 * math.pi / longitudes)
    scaling = 1.0 / math.sqrt(total_count)
    return jnp.stack(
        [jnp.cos(phase_angle) * scaling, -jnp.sin(phase_angle) * scaling], axis=1
    ).astype(jnp.bfloat16)


def damped(spectral, zonal_waves, strength, degrees):
    degree_grid = lax.broadcasted_iota(jnp.int32, spectral.shape, 3)
    component = lax.broadcasted_iota(jnp.int32, spectral.shape, 1)
    zonal_order = zonal_waves[:, None, None, None]
    retained = (degree_grid >= zonal_order) & ((component == 0) | (zonal_order > 0))
    relative = (degree_grid * (degree_grid + 1)).astype(jnp.float32) / float(
        degrees * (degrees + 1)
    )
    factor = 1.0 / (1.0 + strength[None, None, :, None] * relative * relative)
    return jnp.where(retained, spectral.astype(jnp.float32) * factor, 0.0).astype(jnp.bfloat16)


def transport(padded, zonal, meridional):
    centre = padded[1:-1, 1:-1]
    northern = padded[2:, 1:-1]
    southern = padded[:-2, 1:-1]
    eastern = padded[1:-1, 2:]
    western = padded[1:-1, :-2]
    along = (
        centre
        - 0.5 * zonal * (eastern - western)
        + 0.5 * zonal * zonal * (eastern - 2.0 * centre + western)
    )
    return (
        along
        - 0.5 * meridional * (northern - southern)
        + 0.5 * meridional * meridional * (northern - 2.0 * centre + southern)
    )


def clear_poles(padded, depth, lat_dim):
    position = lax.axis_index("lat")
    extent = padded.shape[lat_dim]
    lat_index = lax.broadcasted_iota(jnp.int32, padded.shape, lat_dim)
    lower_rim = (position == 0) & (lat_index < depth)
    upper_rim = (position == lax.axis_size("lat") - 1) & (lat_index >= extent - depth)
    return jnp.where(lower_rim | upper_rim, jnp.zeros_like(padded), padded)


def regime_net(columns, w_in, w_mid, w_out):
    layer_one = jax.nn.silu(
        jnp.einsum("abcl,lh->abch", columns, w_in, preferred_element_type=jnp.float32)
    ).astype(jnp.bfloat16)
    layer_two = jax.nn.silu(
        jnp.einsum("abch,hg->abcg", layer_one, w_mid, preferred_element_type=jnp.float32)
    ).astype(jnp.bfloat16)
    return jnp.einsum("abcg,gl->abcl", layer_two, w_out, preferred_element_type=jnp.float32).astype(
        jnp.bfloat16
    )


def body(
    spectral,
    wavenumber_of_slot,
    filter_strength,
    courant,
    sunlit_blocks,
    sunlit_owner,
    radiation_in,
    radiation_mid,
    radiation_out,
):
    own_count = spectral.shape[0]
    degrees = spectral.shape[3]
    own_waves = lax.dynamic_slice_in_dim(
        wavenumber_of_slot, lax.axis_index("lat") * own_count, own_count
    )
    filtered = damped(spectral, own_waves, filter_strength, degrees)
    coefficients = jnp.einsum(
        "scln,nj->sclj", filtered, latitude_table(degrees, NLAT), preferred_element_type=jnp.float32
    ).astype(jnp.bfloat16)
    wave_table = longitude_table(wavenumber_of_slot, NLON)
    level_slab = jnp.einsum(
        "sclj,sck->jkl",
        lax.all_to_all(coefficients, "lat", split_axis=3, concat_axis=0, tiled=True),
        wave_table,
        preferred_element_type=jnp.float32,
    ).astype(jnp.bfloat16)
    grid_field = lax.all_to_all(level_slab, "lon", split_axis=1, concat_axis=2, tiled=True)
    zonal = courant[0].astype(jnp.float32)
    meridional = courant[1].astype(jnp.float32)
    advected = grid_field.astype(jnp.float32)
    for sweep in range(2):
        padded = clear_poles(
            with_halo(advected.astype(jnp.bfloat16), (("lat", 0), ("lon", 1)), 1).astype(
                advected.dtype
            ),
            1,
            0,
        )
        advected = transport(padded, zonal, meridional)
    state = advected.astype(jnp.bfloat16)
    lat_rows, lon_cols, levels = state.shape
    owners = lax.axis_size("lon")
    blocks = state.reshape(lat_rows * (lon_cols // BC), BC * levels)
    sunlit = sunlit_blocks.reshape(-1)
    destination = sunlit_owner.reshape(-1)
    listed = sunlit.shape[0]
    picked = jnp.take(blocks, sunlit, axis=0)
    position_of = destination * listed + lax.iota(jnp.int32, listed)
    select = (
        position_of[:, None] == lax.broadcasted_iota(jnp.int32, (listed, owners * listed), 1)
    ).astype(jnp.bfloat16)
    outgoing = jnp.einsum("sp,sd->pd", select, picked, preferred_element_type=jnp.float32).astype(
        jnp.bfloat16
    )
    outgoing = outgoing.reshape(owners, listed, BC, levels)
    computed = regime_net(
        lax.all_to_all(outgoing, "lon", split_axis=0, concat_axis=0, tiled=True),
        radiation_in[0],
        radiation_mid[0],
        radiation_out[0],
    )
    returned = lax.all_to_all(computed, "lon", split_axis=0, concat_axis=0, tiled=True).reshape(
        owners * listed, BC * levels
    )
    own_rows = jnp.einsum("sp,pd->sd", select, returned, preferred_element_type=jnp.float32).astype(
        jnp.bfloat16
    )
    covering = (
        sunlit[:, None] == lax.broadcasted_iota(jnp.int32, (listed, blocks.shape[0]), 1)
    ).astype(jnp.bfloat16)
    heating = jnp.einsum(
        "sb,sd->bd", covering, own_rows, preferred_element_type=jnp.float32
    ).astype(jnp.bfloat16)
    return (advected, heating.reshape(lat_rows, lon_cols, levels))


def solution(mesh):
    in_specs = (
        P("lat", None, "lon", None),
        P(),
        P("lon"),
        P(None, "lat", "lon", None),
        P("lat", "lon", None),
        P("lat", "lon", None, None),
        P("lon", None, None),
        P("lon", None, None),
        P("lon", None, None),
    )
    out_specs = (P("lat", "lon", None), P("lat", "lon", None))
    return jax.shard_map(body, mesh=mesh, in_specs=in_specs, out_specs=out_specs, check_vma=False)
```

profile of v0, /device:TPU:32, one launch (start us, length us, event | category | flops | bytes accessed | tf_op | source)
XLA Modules:
  0.0 228.1 jit_solution(16510553503810118711)
XLA Ops:
  0.6 0.0 copy-start
  0.7 0.7 broadcast_multiply_fusion.1
  1.4 0.8 broadcast_compare_fusion
  2.2 8.1 %convolution_convert_fusion.3 = bf16[10,2,8,640]{3,2,1,0:T(8,128)(2,1)} fusion(s32[640]{0:T(1024)S(1)} %get-tuple-element.25, bf16[10,2,8,640]{3,2,1,0:T(8,128)(2,1)} %param.9, f32[640]{0:T(1024)S(1)} %broadcast_multiply_fusion, f32[8]{0:T(128)S(1)} %broadcast_multiply_fusion.1, f32[640]{0:T(1024)S(1)} %get-tuple-element.24, s32[10]{0:T(128)S(1)} %get-tuple-element.11, ...), kind=kOutput, calls=%fused_computation.37 | convolution fusion | flops 136806400 | bytes 417364 | tf_op jit(solution)/shard_map/scln,nj->sclj/dot_general | solution.py:113
  10.3 3.1 %copy.38 = bf16[10,2,8,640]{0,2,1,3:T(8,128)(2,1)S(1)} copy(bf16[10,2,8,640]{3,2,1,0:T(8,128)(2,1)} %convolution_convert_fusion.3) | data formatting | bytes 409600 | tf_op jit(solution)/shard_map/convert_element_type | solution.py:115
  13.4 3.7 %reshape.179 = bf16[64,2,800]{2,1,0:T(2,128)(2,1)} reshape(bf16[640,2,8,10]{3,2,1,0:T(8,128)(2,1)S(1)} %bitcast.100) | data formatting | bytes 409600
  17.0 29.0 %all-to-all-start = ((bf16[64,2,800]{2,1,0:T(2,128)(2,1)}), bf16[64,2,800]{2,1,0:T(2,128)(2,1)S(1)}, u32[]{:S(2)}, u32[]{:S(2)}) async-start(bf16[64,2,800]{2,1,0:T(2,128)(2,1)} %reshape.179), calls=%async_computation | async-start | bytes 458752 | tf_op jit(solution)/shard_map/all_to_all | solution.py:119
  46.1 0.8 fusion.83
  46.9 16.6 %multiply_convert_fusion.3 = (bf16[640,1,1280]{2,0,1:T(8,128)(2,1)}, bf16[640,1,1280]{2,0,1:T(8,128)(2,1)}) fusion(s32[640]{0:T(1024)} %param.10), kind=kLoop, calls=%fused_computation.11 | loop fusion | flops 11468800 | bytes 3279360 | tf_op jit(solution)/shard_map/convert.2
  63.5 22.1 %all-to-all-done = bf16[64,2,800]{2,1,0:T(2,128)(2,1)S(1)} async-done(((bf16[64,2,800]{2,1,0:T(2,128)(2,1)}), bf16[64,2,800]{2,1,0:T(2,128)(2,1)S(1)}, u32[]{:S(2)}, u32[]{:S(2)}) %all-to-all-start) | async-done | bytes 204832 | tf_op jit(solution)/shard_map/all_to_all | solution.py:119
  85.6 3.4 %reshape.180 = bf16[640,2,8,10]{3,2,1,0:T(8,128)(2,1)S(1)} reshape(bf16[64,2,800]{2,1,0:T(2,128)(2,1)S(1)} %all-to-all-done) | data formatting | bytes 409600
  88.9 2.5 %copy.58 = bf16[64,10,2,8,10]{1,0,4,2,3:T(8,128)(2,1)} copy(bf16[64,10,2,8,10]{1,3,2,4,0:T(8,128)(2,1)S(1)} %bitcast.101) | data formatting | bytes 409600 | tf_op jit(solution)/shard_map/all_to_all | solution.py:119
  91.4 4.6 %reshape.178 = bf16[640,2,8,10]{0,3,1,2:T(8,128)(2,1)S(1)} reshape(bf16[64,10,2,8,10]{1,0,4,2,3:T(8,128)(2,1)} %copy.58) | data formatting | bytes 409600 | tf_op jit(solution)/shard_map/all_to_all | solution.py:119
  96.1 2.5 %fusion.14 = bf16[10,1280,8]{1,0,2:T(8,128)(2,1)S(1)} fusion(bf16[640,2,8,10]{0,3,1,2:T(8,128)(2,1)S(1)} %reshape.178, bf16[640,1,1280]{2,0,1:T(8,128)(2,1)} %get-tuple-element.23, bf16[640,1,1280]{2,0,1:T(8,128)(2,1)} %get-tuple-element.22), kind=kOutput, calls=%fused_computation.23 | convolution fusion | flops 268800000 | bytes 3686400 | tf_op jit(solution)/shard_map/sclj,sck->jkl/dot_general | solution.py:117
  98.6 0.0 copy-start.2
  98.6 1.9 copy.42
  100.5 5.5 %reshape.181 = bf16[16,2,3200]{2,1,0:T(2,128)(2,1)} reshape(bf16[1280,8,10]{2,1,0:T(8,128)(2,1)S(1)} %bitcast.102) | data formatting | bytes 409600
  106.0 7.0 %all-to-all-start.1 = ((bf16[16,2,3200]{2,1,0:T(2,128)(2,1)}), bf16[16,2,3200]{2,1,0:T(2,128)(2,1)S(1)}, u32[]{:S(2)}, u32[]{:S(2)}) async-start(bf16[16,2,3200]{2,1,0:T(2,128)(2,1)} %reshape.181), calls=%async_computation.1 | async-start | bytes 409600 | tf_op jit(solution)/shard_map/all_to_all | solution.py:123
  113.1 8.1 %all-to-all-done.1 = bf16[16,2,3200]{2,1,0:T(2,128)(2,1)S(1)} async-done(((bf16[16,2,3200]{2,1,0:T(2,128)(2,1)}), bf16[16,2,3200]{2,1,0:T(2,128)(2,1)S(1)}, u32[]{:S(2)}, u32[]{:S(2)}) %all-to-all-start.1) | async-done | bytes 204832 | tf_op jit(solution)/shard_map/all_to_all | solution.py:123
  121.2 6.2 %reshape.182 = bf16[1280,8,10]{2,1,0:T(8,128)(2,1)S(1)} reshape(bf16[16,2,3200]{2,1,0:T(2,128)(2,1)S(1)} %all-to-all-done.1) | data formatting | bytes 409600
  127.5 2.0 copy.59
  129.5 0.6 copy.74
  130.1 0.6 copy.73
  130.8 0.0 collective-permute-start.1
  130.8 0.5 collective-permute-start
  131.3 1.7 copy.45
  133.0 1.3 collective-permute-done
  134.3 0.1 pad_maximum_fusion
  134.4 0.2 fusion.85
  134.6 2.5 %collective-permute-start.2 = (bf16[12,1,128]{1,2,0:T(8,128)(2,1)S(1)}, bf16[12,1,128]{1,2,0:T(8,128)(2,1)S(1)}, u32[]{:S(2)}, u32[]{:S(2)}) collective-permute-start(bf16[12,1,128]{1,2,0:T(8,128)(2,1)S(1)} %get-tuple-element.16), channel_id=1, source_target_pairs={{0,1},{1,2},{2,3},{3,4},{4,5},{5,6},{6,7},{7,8},{8,9},{9,10},{10,1... | collective-permute-start | bytes 9224 | tf_op jit(solution)/shard_map/ppermute | solution.py:20
  137.1 6.7 %collective-permute-start.3 = (bf16[12,1,128]{1,2,0:T(8,128)(2,1)S(1)}, bf16[12,1,128]{1,2,0:T(8,128)(2,1)S(1)}, u32[]{:S(2)}, u32[]{:S(2)}) collective-permute-start(bf16[12,1,128]{1,2,0:T(8,128)(2,1)S(1)} %get-tuple-element.17), channel_id=1, source_target_pairs={{1,0},{2,1},{3,2},{4,3},{5,4},{6,5},{7,6},{8,7},{9,8},{10,9},{11,1... | collective-permute-start | bytes 9224 | tf_op jit(solution)/shard_map/ppermute | solution.py:21
  143.8 1.1 copy.62
  145.0 1.2 copy.63
  146.1 0.0 copy-start.5
  146.1 3.4 %collective-permute-done.2 = bf16[12,1,128]{1,2,0:T(8,128)(2,1)S(1)} collective-permute-done((bf16[12,1,128]{1,2,0:T(8,128)(2,1)S(1)}, bf16[12,1,128]{1,2,0:T(8,128)(2,1)S(1)}, u32[]{:S(2)}, u32[]{:S(2)}) %collective-permute-start.2) | collective-permute-done | bytes 3104 | tf_op jit(solution)/shard_map/ppermute | solution.py:20
  149.6 1.2 collective-permute-done.3
  150.7 0.4 convert_select_fusion.1
  151.1 0.7 fusion.41
  151.9 0.0 collective-permute-start.4
  151.9 1.7 collective-permute-start.5
  153.7 1.6 collective-permute-done.4
  155.2 0.0 collective-permute-done.5
  155.3 0.1 pad_maximum_fusion.1
  155.3 0.2 fusion.84
  155.5 1.9 collective-permute-start.6
  157.5 7.7 %collective-permute-start.7 = (bf16[12,1,128]{1,2,0:T(8,128)(2,1)S(1)}, bf16[12,1,128]{1,2,0:T(8,128)(2,1)S(1)}, u32[]{:S(2)}, u32[]{:S(2)}) collective-permute-start(bf16[12,1,128]{1,2,0:T(8,128)(2,1)S(1)} %get-tuple-element.15), channel_id=1, source_target_pairs={{1,0},{2,1},{3,2},{4,3},{5,4},{6,5},{7,6},{8,7},{9,8},{10,9},{11,1... | collective-permute-start | bytes 9224 | tf_op jit(solution)/shard_map/ppermute | solution.py:21
  165.2 8.0 %collective-permute-done.6 = bf16[12,1,128]{1,2,0:T(8,128)(2,1)S(1)} collective-permute-done((bf16[12,1,128]{1,2,0:T(8,128)(2,1)S(1)}, bf16[12,1,128]{1,2,0:T(8,128)(2,1)S(1)}, u32[]{:S(2)}, u32[]{:S(2)}) %collective-permute-start.6) | collective-permute-done | bytes 3104 | tf_op jit(solution)/shard_map/ppermute | solution.py:20
  173.2 1.3 collective-permute-done.7
  174.5 0.4 convert_select_fusion
  174.8 0.7 fusion.81
  175.6 0.0 copy-start.3
  175.6 0.2 copy.49
  175.8 0.1 reshape.157
  175.9 0.6 gather_fusion
  176.5 0.5 fusion.24
  177.0 0.2 copy.64
  177.1 21.2 %all_to_all.46 = bf16[16,12,16,128]{3,2,1,0:T(8,128)(2,1)S(1)} all-to-all(bf16[16,12,16,128]{3,2,1,0:T(8,128)(2,1)S(1)} %bitcast.104), channel_id=1, replica_groups=mesh['lat'=64,'lon'=16] {'lon'}, dimensions={0} | all-to-all | bytes 1572864 | tf_op jit(solution)/shard_map/all_to_all | solution.py:153
  198.3 6.0 %fusion.8 = f32[16,12,16,512]{3,2,1,0:T(8,128)} fusion(bf16[16,12,16,128]{3,2,1,0:T(8,128)(2,1)S(1)} %all_to_all.46, bf16[1,512,512]{2,1,0:T(8,128)(2,1)S(1)} %copy-done, bf16[1,128,512]{2,1,0:T(8,128)(2,1)S(1)} %copy-done.3), kind=kOutput, calls=%fused_computation.16 | convolution fusion | flops 2021130240 | bytes 7733248 | tf_op jit(solution)/shard_map/abch,hg->abcg/dot_general | solution.py:89
  204.3 5.5 %fusion.23 = bf16[16,12,16,128]{3,2,1,0:T(8,128)(2,1)} fusion(f32[16,12,16,512]{3,2,1,0:T(8,128)} %fusion.8, bf16[1,512,128]{2,1,0:T(8,128)(2,1)S(1)} %copy-done.4), kind=kOutput, calls=%fused_computation.35 | convolution fusion | flops 410910720 | bytes 7208960 | tf_op jit(solution)/shard_map/abcg,gl->abcl/dot_general | solution.py:91
  209.8 3.7 %all-to-all-start.3 = ((bf16[16,12,16,128]{3,2,1,0:T(8,128)(2,1)}), bf16[16,12,16,128]{3,2,1,0:T(8,128)(2,1)S(1)}, u32[]{:S(2)}, u32[]{:S(2)}) async-start(bf16[16,12,16,128]{3,2,1,0:T(8,128)(2,1)} %fusion.23), calls=%async_computation.3 | async-start | bytes 1572864 | tf_op jit(solution)/shard_map/all_to_all | solution.py:158
  213.4 1.0 copy.50
  214.4 12.4 %all-to-all-done.3 = bf16[16,12,16,128]{3,2,1,0:T(8,128)(2,1)S(1)} async-done(((bf16[16,12,16,128]{3,2,1,0:T(8,128)(2,1)}), bf16[16,12,16,128]{3,2,1,0:T(8,128)(2,1)S(1)}, u32[]{:S(2)}, u32[]{:S(2)}) %all-to-all-start.3) | async-done | bytes 786464 | tf_op jit(solution)/shard_map/all_to_all | solution.py:158
  226.8 0.4 convolution_convert_fusion.1
  227.3 0.8 reshape.161
  (19 shorter events, 0.1 us)
Async XLA Ops:
  0.6 197.7 %copy-start = (bf16[1,512,512]{2,1,0:T(8,128)(2,1)S(1)}, bf16[1,512,512]{2,1,0:T(8,128)(2,1)}, u32[]{:S(2)}) copy-start(bf16[1,512,512]{2,1,0:T(8,128)(2,1)} %param.16) | copy-start | bytes 1572868
  10.3 35.8 %copy-start.1 = (bf16[2,10,80,128]{3,2,1,0:T(8,128)(2,1)S(1)}, bf16[2,10,80,128]{3,2,1,0:T(8,128)(2,1)}, u32[]{:S(2)}) copy-start(bf16[2,10,80,128]{3,2,1,0:T(8,128)(2,1)} %param.12) | copy-start | bytes 1228804
  17.0 68.5 %all-to-all-start = ((bf16[64,2,800]{2,1,0:T(2,128)(2,1)}), bf16[64,2,800]{2,1,0:T(2,128)(2,1)S(1)}, u32[]{:S(2)}, u32[]{:S(2)}) async-start(bf16[64,2,800]{2,1,0:T(2,128)(2,1)} %reshape.179), calls=%async_computation | async-start | bytes 458752 | tf_op jit(solution)/shard_map/all_to_all | solution.py:119
  98.6 14.5 %copy-start.2 = (s32[1,1,12]{2,1,0:T(1,128)S(1)}, s32[1,1,12]{2,1,0:T(1,128)}, u32[]{:S(2)}) copy-start(s32[1,1,12]{2,1,0:T(1,128)} %param.13) | copy-start | bytes 148
  106.0 15.2 %all-to-all-start.1 = ((bf16[16,2,3200]{2,1,0:T(2,128)(2,1)}), bf16[16,2,3200]{2,1,0:T(2,128)(2,1)S(1)}, u32[]{:S(2)}, u32[]{:S(2)}) async-start(bf16[16,2,3200]{2,1,0:T(2,128)(2,1)} %reshape.181), calls=%async_computation.1 | async-start | bytes 409600 | tf_op jit(solution)/shard_map/all_to_all | solution.py:123
  130.8 2.3 collective-permute-start.1
  130.8 3.6 %collective-permute-start = (bf16[1,80,128]{1,2,0:T(8,128)(2,1)}, bf16[1,80,128]{1,2,0:T(8,128)(2,1)S(1)}, u32[]{:S(2)}, u32[]{:S(2)}) collective-permute-start(bf16[1,80,128]{1,2,0:T(8,128)(2,1)} %bitcast.97), channel_id=1, source_target_pairs={{0,16},{16,32},{32,48},{48,64},{64,80},{80,96},{96,112},{112,128},... | collective-permute-start | bytes 61448 | tf_op jit(solution)/shard_map/ppermute | solution.py:20
  134.6 15.0 %collective-permute-start.2 = (bf16[12,1,128]{1,2,0:T(8,128)(2,1)S(1)}, bf16[12,1,128]{1,2,0:T(8,128)(2,1)S(1)}, u32[]{:S(2)}, u32[]{:S(2)}) collective-permute-start(bf16[12,1,128]{1,2,0:T(8,128)(2,1)S(1)} %get-tuple-element.16), channel_id=1, source_target_pairs={{0,1},{1,2},{2,3},{3,4},{4,5},{5,6},{6,7},{7,8},{8,9},{9,10},{10,1... | collective-permute-start | bytes 9224 | tf_op jit(solution)/shard_map/ppermute | solution.py:20
  137.1 13.7 %collective-permute-start.3 = (bf16[12,1,128]{1,2,0:T(8,128)(2,1)S(1)}, bf16[12,1,128]{1,2,0:T(8,128)(2,1)S(1)}, u32[]{:S(2)}, u32[]{:S(2)}) collective-permute-start(bf16[12,1,128]{1,2,0:T(8,128)(2,1)S(1)} %get-tuple-element.17), channel_id=1, source_target_pairs={{1,0},{2,1},{3,2},{4,3},{5,4},{6,5},{7,6},{8,7},{9,8},{10,9},{11,1... | collective-permute-start | bytes 9224 | tf_op jit(solution)/shard_map/ppermute | solution.py:21
  146.1 7.5 %copy-start.5 = (s32[1,1,12,1]{2,3,1,0:T(1,128)S(1)}, s32[1,1,12,1]{2,3,1,0:T(1,128)}, u32[]{:S(2)}) copy-start(s32[1,1,12,1]{2,3,1,0:T(1,128)} %param.14) | copy-start | bytes 148
  151.9 3.4 %collective-permute-start.4 = (bf16[1,80,128]{1,2,0:T(8,128)(2,1)S(1)}, bf16[1,80,128]{1,2,0:T(8,128)(2,1)S(1)}, u32[]{:S(2)}, u32[]{:S(2)}) collective-permute-start(bf16[1,80,128]{1,2,0:T(8,128)(2,1)S(1)} %get-tuple-element.18), channel_id=1, source_target_pairs={{0,16},{16,32},{32,48},{48,64},{64,80},{80,96},{96,112},{112,128},... | collective-permute-start | bytes 61448 | tf_op jit(solution)/shard_map/ppermute | solution.py:20
  151.9 3.3 %collective-permute-start.5 = (bf16[1,80,128]{1,2,0:T(8,128)(2,1)S(1)}, bf16[1,80,128]{1,2,0:T(8,128)(2,1)S(1)}, u32[]{:S(2)}, u32[]{:S(2)}) collective-permute-start(bf16[1,80,128]{1,2,0:T(8,128)(2,1)S(1)} %get-tuple-element.19), channel_id=1, source_target_pairs={{16,0},{32,16},{48,32},{64,48},{80,64},{96,80},{112,96},{128,112},... | collective-permute-start | bytes 61448 | tf_op jit(solution)/shard_map/ppermute | solution.py:21
  155.5 17.6 %collective-permute-start.6 = (bf16[12,1,128]{1,2,0:T(8,128)(2,1)S(1)}, bf16[12,1,128]{1,2,0:T(8,128)(2,1)S(1)}, u32[]{:S(2)}, u32[]{:S(2)}) collective-permute-start(bf16[12,1,128]{1,2,0:T(8,128)(2,1)S(1)} %get-tuple-element.14), channel_id=1, source_target_pairs={{0,1},{1,2},{2,3},{3,4},{4,5},{5,6},{6,7},{7,8},{8,9},{9,10},{10,1... | collective-permute-start | bytes 9224 | tf_op jit(solution)/shard_map/ppermute | solution.py:20
  157.5 17.0 %collective-permute-start.7 = (bf16[12,1,128]{1,2,0:T(8,128)(2,1)S(1)}, bf16[12,1,128]{1,2,0:T(8,128)(2,1)S(1)}, u32[]{:S(2)}, u32[]{:S(2)}) collective-permute-start(bf16[12,1,128]{1,2,0:T(8,128)(2,1)S(1)} %get-tuple-element.15), channel_id=1, source_target_pairs={{1,0},{2,1},{3,2},{4,3},{5,4},{6,5},{7,6},{8,7},{9,8},{10,9},{11,1... | collective-permute-start | bytes 9224 | tf_op jit(solution)/shard_map/ppermute | solution.py:21
  175.6 22.7 %copy-start.3 = (bf16[1,128,512]{2,1,0:T(8,128)(2,1)S(1)}, bf16[1,128,512]{2,1,0:T(8,128)(2,1)}, u32[]{:S(2)}) copy-start(bf16[1,128,512]{2,1,0:T(8,128)(2,1)} %param.15) | copy-start | bytes 393220
  198.3 6.0 %copy-start.4 = (bf16[1,512,128]{2,1,0:T(8,128)(2,1)S(1)}, bf16[1,512,128]{2,1,0:T(8,128)(2,1)}, u32[]{:S(2)}) copy-start(bf16[1,512,128]{2,1,0:T(8,128)(2,1)} %param.17) | copy-start | bytes 393220
  209.8 17.1 %all-to-all-start.3 = ((bf16[16,12,16,128]{3,2,1,0:T(8,128)(2,1)}), bf16[16,12,16,128]{3,2,1,0:T(8,128)(2,1)S(1)}, u32[]{:S(2)}, u32[]{:S(2)}) async-start(bf16[16,12,16,128]{3,2,1,0:T(8,128)(2,1)} %fusion.23), calls=%async_computation.3 | async-start | bytes 1572864 | tf_op jit(solution)/shard_map/all_to_all | solution.py:158
where the time goes:
time: 229 us; the launch traced here: 228 us
  starting transfers between devices  60.8 us (27%)
  waiting for transfers between devices  59.3 us (26%)
  local copies, waits for them, and re-layouts  42.2 us (18%)
  matrix products  23 us (10%)
  blocking collectives  21.2 us (9%)
  other arithmetic  20.6 us (9%)
    all_to_all x1, starting transfers between devices, body(): lax.all_to_all(coefficients, 'lat', split_axis=3, concat_axis=0, tiled=True)  29 us
    unnamed x20, local copies, waits for them, and re-layouts  22.2 us
    all_to_all x1, waiting for transfers between devices, body(): lax.all_to_all(coefficients, 'lat', split_axis=3, concat_axis=0, tiled=True)  22.1 us
    all_to_all x1, blocking collectives, body(): lax.all_to_all(outgoing, 'lon', split_axis=0, concat_axis=0, tiled=True)  21.2 us
    another operation x1, other arithmetic  16.6 us
    ppermute x4, starting transfers between devices, with_halo(): after = lax.ppermute(leading, axis, down)  16.2 us
    ppermute x4, waiting for transfers between devices, with_halo(): before = lax.ppermute(last, axis, up)  14.3 us
    all_to_all x1, waiting for transfers between devices, body(): lax.all_to_all(computed, 'lon', split_axis=0, concat_axis=0, tiled=True)  12.4 us
  transfers between devices with their start and end apart: 11, of which 9 were waited for; matrix products, arithmetic and copies ran while one was open for 10% of the time, Pallas kernels for 0%

commit v1 on v0

v1 whole, which is shorter than its diff:
```python
import functools
import math

import jax
import jax.numpy as jnp
import numpy as np
from jax import lax
from jax.experimental import pallas as pl
from jax.experimental.pallas import tpu as pltpu
from jax.sharding import PartitionSpec as P

MESH = pl.DeviceIdType.MESH
F32 = jnp.float32
BF16 = jnp.bfloat16

DEG = 640
NLON = 1280
LAT = 64
LON = 16
ROWS = 10
COLS = 80
LEV = 128
OWN = 8
LEAD = 8
WIDE = 96
HID = 512


def latitude_rows():
    row = np.arange(LAT * 16) % 16
    j = np.arange(LAT * 16) // 16 * ROWS + np.where(row < ROWS, row, row - ROWS)
    n = np.arange(DEG)
    phase = (n[None, :] * (2 * j[:, None] + 1)) % (4 * DEG)
    table = np.cos(phase * (math.pi / (2.0 * DEG))) * math.sqrt(2.0 / DEG)
    return table.astype(np.float32).astype(jnp.bfloat16)


def circle(turns):
    y = turns * math.pi
    z = y * y
    s = 1.0
    for k in (11, 9, 7, 5, 3):
        s = 1.0 - z * s * (1.0 / (k * (k - 1)))
    s = s * y
    c = 1.0
    for k in (12, 10, 8, 6, 4, 2):
        c = 1.0 - z * c * (1.0 / (k * (k - 1)))
    return 1.0 - 2.0 * s * s, 2.0 * s * c


def fraction(product):
    turns = product * (1.0 / NLON)
    return turns - jnp.floor(turns + 0.5)


def silu(v):
    return v / (1.0 + jnp.exp(-v))


def peer_at(t, p):
    i = t // 2
    far = 16 - (i + 1) // 2
    chip = lax.rem(p // 2 + jnp.where(i % 2 == 1, far, 32 - far), 32)
    core = jnp.where(t == 62, 1 - lax.rem(p, 2), lax.rem(t, 2))
    return jnp.where(t == 62, p // 2, chip) * 2 + core


def kernel(
    wave_ref,
    strength_ref,
    sunlit_ref,
    owner_ref,
    spectral_hbm,
    table_hbm,
    courant_hbm,
    win_hbm,
    wmid_hbm,
    wout_hbm,
    advected_hbm,
    heating_hbm,
    spec,
    table,
    cour,
    w_in,
    w_mid,
    w_out,
    damp,
    pay,
    got,
    gotf,
    wide,
    trig,
    mcol,
    slab,
    land,
    c_north,
    c_south,
    c_west,
    c_east,
    flow,
    q_zero,
    q_one,
    adv,
    state,
    out_slots,
    in_slots,
    back_slots,
    ret_slots,
    heat,
    pick,
    place,
    local_sem,
    send_sem,
    recv_sem,
):
    p = lax.axis_index("lat")
    q = lax.axis_index("lon")
    north = lax.rem(p + 1, LAT)
    south = lax.rem(p + LAT - 1, LAT)
    east = lax.rem(q + 1, LON)
    west = lax.rem(q + LON - 1, LON)

    get_spec = pltpu.make_async_copy(spectral_hbm, spec, local_sem.at[0])
    get_table = pltpu.make_async_copy(table_hbm, table, local_sem.at[1])
    get_cour = pltpu.make_async_copy(courant_hbm, cour, local_sem.at[2])
    get_in = pltpu.make_async_copy(win_hbm, w_in, local_sem.at[3])
    get_mid = pltpu.make_async_copy(wmid_hbm, w_mid, local_sem.at[4])
    get_out = pltpu.make_async_copy(wout_hbm, w_out, local_sem.at[5])
    get_spec.start()
    get_table.start()

    barrier = pltpu.get_barrier_semaphore()

    def greet_lat(t, carry):
        pl.semaphore_signal(barrier, inc=1, device_id=(peer_at(t, p), q), device_id_type=MESH)
        return carry

    lax.fori_loop(0, LAT - 1, greet_lat, 0)

    def greet_lon(t, carry):
        other = lax.rem(q + t, LON)
        for row in (p, north, south):
            pl.semaphore_signal(barrier, inc=1, device_id=(row, other), device_id_type=MESH)
        return carry

    lax.fori_loop(1, LON, greet_lon, 0)

    get_cour.start()
    get_in.start()
    get_mid.start()
    get_out.start()

    degree = lax.broadcasted_iota(jnp.int32, (OWN, DEG), 1)
    level = lax.broadcasted_iota(jnp.int32, (OWN, DEG), 0)
    strength = jnp.zeros((OWN, DEG), F32)
    for l in range(OWN):
        strength = jnp.where(level == l, strength_ref[l], strength)
    relative = (degree * (degree + 1)).astype(F32) / float(DEG * (DEG + 1))
    factor = 1.0 / (1.0 + strength * relative * relative)
    get_spec.wait()
    for s in range(ROWS):
        wave = wave_ref[p * ROWS + s]
        real = jnp.where(degree >= wave, spec[s, 0].astype(F32) * factor, 0.0)
        imag = jnp.where(
            degree >= jnp.where(wave > 0, wave, DEG), spec[s, 1].astype(F32) * factor, 0.0
        )
        both = jnp.concatenate([real, imag], axis=0).astype(BF16)
        damp[pl.ds(s * 16, 16), :] = both
        if s >= 8:
            damp[pl.ds(s * 16 + 32, 16), :] = both
    damp[pl.ds(192, 64), :] = jnp.zeros((64, DEG), BF16)

    get_table.wait()
    row16 = lax.broadcasted_iota(jnp.int32, (128, LEV), 0) % 16
    lane = lax.broadcasted_iota(jnp.int32, (128, LEV), 1)

    def over_degrees(t, carry):
        rows = table[pl.ds(pl.multiple_of(t * 128, 128), 128), :]
        y = lax.dot_general(rows, damp[...], (((1,), (1,)), ((), ())), preferred_element_type=F32)
        first, last = y[:, :128], y[:, 128:]
        tail = jnp.where(lane < 32, last, pltpu.roll(last, 6, 0))
        packed = jnp.where(row16 < ROWS, first, tail).astype(BF16)
        pay[pl.ds(t * 8, 8)] = packed.reshape(8, 16, LEV)
        return carry

    lax.fori_loop(0, 8, over_degrees, 0)

    sub8 = lax.broadcasted_iota(jnp.int32, (8, LEV), 0)

    def columns(t, carry):
        s, group = t // 8, lax.rem(t, 8)
        value = jnp.zeros((8, LEV), jnp.int32)
        for r in range(8):
            value = jnp.where(sub8 == r, wave_ref[(group * 8 + r) * ROWS + s], value)
        mcol[pl.ds(pl.multiple_of(t * 8, 8), 8), :] = value.astype(F32)
        return carry

    lax.fori_loop(0, 80, columns, 0)

    shift = (lax.broadcasted_iota(jnp.int32, (64, LEV), 1) - LEAD).astype(F32)
    scale = 1.0 / math.sqrt(DEG)

    def trig_rows(s, carry):
        m = mcol[pl.ds(pl.multiple_of(s * 64, 64), 64), :]
        c, d = circle(fraction(m * shift))
        c, d = c * scale, d * scale
        c1, d1 = circle(fraction(m * float(COLS)))
        base = pl.multiple_of(s * 128, 128)
        for other in range(LON):
            lanes = pl.ds((other % 2) * 128, 128)
            trig[other // 2, pl.ds(base, 64), lanes] = c.astype(BF16)
            trig[other // 2, pl.ds(base + 64, 64), lanes] = (-d).astype(BF16)
            c, d = c * c1 - d * d1, d * c1 + c * d1
        return carry

    lax.fori_loop(0, ROWS, trig_rows, 0)

    def clear_pick(t, carry):
        pick[t] = 0
        return carry

    owners = [owner_ref[t] for t in range(12)]
    listed = [sunlit_ref[t] for t in range(12)]
    slots = []
    for t in range(12):
        rank = jnp.int32(0)
        for u in range(t):
            rank = rank + (owners[u] == owners[t]).astype(jnp.int32)
        slots.append(owners[t] * 2 + rank)

    def fill_pick(k, carry):
        value = jnp.int32(0)
        for t in range(12):
            value = jnp.where(slots[t] == k, listed[t], value)
        pick[k] = value
        return carry

    lax.fori_loop(0, 32, fill_pick, 0)

    def fill_place(k, carry):
        value = jnp.int32(32)
        for t in range(12):
            value = jnp.where(listed[t] == k, slots[t], value)
        place[k] = value
        return carry

    lax.fori_loop(0, 50, fill_place, 0)

    get_cour.wait()
    pl.semaphore_wait(barrier, LAT - 1 + 3 * (LON - 1))

    def send_lat(t, carry):
        other = peer_at(t, p)
        pltpu.make_async_remote_copy(
            pay.at[other],
            got.at[p],
            send_sem.at[0],
            recv_sem.at[0],
            device_id=(other, q),
            device_id_type=MESH,
        ).start()
        return carry

    lax.fori_loop(0, LAT - 1, send_lat, 0)
    pltpu.make_async_copy(pay.at[p], got.at[p], recv_sem.at[0]).start()

    edges = [
        pltpu.make_async_remote_copy(
            cour.at[:, ROWS - 1],
            c_south,
            send_sem.at[1],
            recv_sem.at[1],
            device_id=(north, q),
            device_id_type=MESH,
        ),
        pltpu.make_async_remote_copy(
            cour.at[:, 0],
            c_north,
            send_sem.at[2],
            recv_sem.at[2],
            device_id=(south, q),
            device_id_type=MESH,
        ),
        pltpu.make_async_remote_copy(
            cour.at[:, :, pl.ds(COLS - 16, 16), :],
            c_west,
            send_sem.at[3],
            recv_sem.at[3],
            device_id=(p, east),
            device_id_type=MESH,
        ),
        pltpu.make_async_remote_copy(
            cour.at[:, :, pl.ds(0, 16), :],
            c_east,
            send_sem.at[4],
            recv_sem.at[4],
            device_id=(p, west),
            device_id_type=MESH,
        ),
    ]
    for edge in edges:
        edge.start()
    for edge in edges:
        edge.wait()
    zeros8 = jnp.zeros((8, LEV), F32)
    for k in range(2):
        flow[k, 0] = jnp.concatenate([zeros8, c_south[k].astype(F32), zeros8], axis=0)
        flow[k, ROWS + 1] = jnp.concatenate([zeros8, c_north[k].astype(F32), zeros8], axis=0)

    def fill_flow(r, carry):
        for k in range(2):
            flow[k, r + 1] = jnp.concatenate(
                [
                    c_west[k, r].astype(F32)[8:],
                    cour[k, r].astype(F32),
                    c_east[k, r].astype(F32)[:8],
                ],
                axis=0,
            )
        return carry

    lax.fori_loop(0, ROWS, fill_flow, 0)

    pltpu.make_async_copy(got, got, recv_sem.at[0]).wait()
    gotf[...] = got[...].astype(F32).reshape(LAT * 16, LEV)
    low = lax.broadcasted_iota(jnp.int32, (8, LEV), 1) < 64
    for r in range(16):
        part = gotf[pl.ds(r, LAT, stride=16), :]
        turned = jnp.concatenate([part, part], axis=0).T
        if r < ROWS:
            for a in range(8):
                wide[pl.ds(r * 8, 8), pl.ds(a * 128, 128)] = jnp.where(
                    low, turned[a * 16 : a * 16 + 8], turned[a * 16 + 8 : a * 16 + 16]
                )
        else:
            for g, jj in ((0, r - ROWS), (1, r - ROWS + 4)):
                if g == 1 and jj < 6:
                    continue
                for a in range(2):
                    at = g * 32 + a * 16
                    wide[pl.ds(jj * 8, 8), pl.ds((8 + a) * 128, 128)] = jnp.where(
                        low, turned[at : at + 8], turned[at + 8 : at + 16]
                    )

    def send_lon(t, carry):
        pair = lax.rem(q // 2 + t, LON // 2)
        g = jnp.dot(wide[...].astype(BF16), trig[pair], preferred_element_type=F32).astype(BF16)
        for h in range(2):
            other = pair * 2 + h
            slab[other] = g[:, h * 128 : (h + 1) * 128]

            @pl.when(other != q)
            def _():
                pltpu.make_async_remote_copy(
                    slab.at[other],
                    land.at[q, pl.ds(16, 80), :],
                    send_sem.at[5],
                    recv_sem.at[5],
                    device_id=(p, other),
                    device_id_type=MESH,
                ).start()

            @pl.when(other == q)
            def _():
                pltpu.make_async_copy(
                    slab.at[other], land.at[q, pl.ds(16, 80), :], recv_sem.at[5]
                ).start()

            pltpu.make_async_remote_copy(
                slab.at[other, pl.ds(64, 16), :],
                land.at[q, pl.ds(0, 16), :],
                send_sem.at[5],
                recv_sem.at[5],
                device_id=(north, other),
                device_id_type=MESH,
            ).start()
            pltpu.make_async_remote_copy(
                slab.at[other, pl.ds(0, 16), :],
                land.at[q, pl.ds(96, 16), :],
                send_sem.at[5],
                recv_sem.at[5],
                device_id=(south, other),
                device_id_type=MESH,
            ).start()
        return carry

    lax.fori_loop(0, LON // 2, send_lon, 0)
    pltpu.make_async_copy(land, land, recv_sem.at[5]).wait()

    for h in range(7):
        two = land[:, pl.ds(h * 16, 16), :].astype(F32)
        for k in range(2):
            field = two[:, k * 8 : k * 8 + 8, :].reshape(128, 128).T[:WIDE]
            if h == 0:
                field = jnp.where(p == 0, 0.0, field)
            if h == 6:
                field = jnp.where(p == LAT - 1, 0.0, field)
            q_zero[h * 2 + k] = field

    def step(centre, upper, lower, u, v):
        right = pltpu.roll(centre, WIDE - 1, 0)
        left = pltpu.roll(centre, 1, 0)
        along = centre - 0.5 * u * (right - left) + 0.5 * u * u * (right - 2.0 * centre + left)
        return (
            along - 0.5 * v * (upper - lower) + 0.5 * v * v * (upper - 2.0 * centre + lower)
        )

    def first_step(r, carry):
        q_one[r] = step(q_zero[r + 1], q_zero[r + 2], q_zero[r], flow[0, r], flow[1, r])
        return carry

    lax.fori_loop(0, ROWS + 2, first_step, 0)
    q_one[0] = jnp.where(p == 0, 0.0, q_one[0])
    q_one[ROWS + 1] = jnp.where(p == LAT - 1, 0.0, q_one[ROWS + 1])

    def second_step(r, carry):
        new = step(q_one[r + 1], q_one[r + 2], q_one[r], flow[0, r + 1], flow[1, r + 1])
        new = new[LEAD : LEAD + COLS]
        adv[r] = new
        state[pl.ds(r * 5, 5)] = new.astype(BF16).reshape(5, 16, LEV)
        return carry

    lax.fori_loop(0, ROWS, second_step, 0)
    put_adv = pltpu.make_async_copy(adv, advected_hbm, local_sem.at[6])
    put_adv.start()

    def pack(k, carry):
        out_slots[k] = state[pick[k]]
        return carry

    lax.fori_loop(0, 2 * LON, pack, 0)

    def send_out(t, carry):
        other = lax.rem(q + t, LON)
        pltpu.make_async_remote_copy(
            out_slots.at[pl.ds(other * 2, 2)],
            in_slots.at[pl.ds(q * 2, 2)],
            send_sem.at[6],
            recv_sem.at[6],
            device_id=(p, other),
            device_id_type=MESH,
        ).start()
        return carry

    lax.fori_loop(1, LON, send_out, 0)
    pltpu.make_async_copy(
        out_slots.at[pl.ds(q * 2, 2)], in_slots.at[pl.ds(q * 2, 2)], recv_sem.at[6]
    ).start()
    get_in.wait()
    get_mid.wait()
    get_out.wait()
    pltpu.make_async_copy(in_slots, in_slots, recv_sem.at[6]).wait()
    x = in_slots[...].reshape(HID, LEV)
    one = silu(jnp.dot(x, w_in[0], preferred_element_type=F32)).astype(BF16)
    two = silu(jnp.dot(one, w_mid[0], preferred_element_type=F32)).astype(BF16)
    three = jnp.dot(two, w_out[0], preferred_element_type=F32).astype(BF16)
    back_slots[...] = three.reshape(2 * LON, 16, LEV)

    def send_back(t, carry):
        other = lax.rem(q + t, LON)
        pltpu.make_async_remote_copy(
            back_slots.at[pl.ds(other * 2, 2)],
            ret_slots.at[pl.ds(q * 2, 2)],
            send_sem.at[7],
            recv_sem.at[7],
            device_id=(p, other),
            device_id_type=MESH,
        ).start()
        return carry

    lax.fori_loop(1, LON, send_back, 0)
    pltpu.make_async_copy(
        back_slots.at[pl.ds(q * 2, 2)], ret_slots.at[pl.ds(q * 2, 2)], recv_sem.at[7]
    ).start()
    ret_slots[2 * LON] = jnp.zeros((16, LEV), BF16)
    some = pl.ds(0, 2 * LON)
    pltpu.make_async_copy(ret_slots.at[some], ret_slots.at[some], recv_sem.at[7]).wait()

    def unpack(r, carry):
        for k in range(5):
            heat[r, pl.ds(k * 16, 16), :] = ret_slots[place[r * 5 + k]]
        return carry

    lax.fori_loop(0, ROWS, unpack, 0)
    put_heat = pltpu.make_async_copy(heat, heating_hbm, local_sem.at[7])
    put_heat.start()

    sent = pl.ds(0, LAT - 1)
    pltpu.make_async_copy(pay.at[sent], pay.at[sent], send_sem.at[0]).wait()
    sent = pl.ds(0, LON - 1)
    pltpu.make_async_copy(slab.at[sent], slab.at[sent], send_sem.at[5]).wait()
    sent = pl.ds(0, 2 * LON)
    edge_rows = slab.at[pl.ds(0, LON), pl.ds(0, 32), :]
    pltpu.make_async_copy(edge_rows, edge_rows, send_sem.at[5]).wait()
    sent = pl.ds(0, 2 * LON - 2)
    pltpu.make_async_copy(out_slots.at[sent], out_slots.at[sent], send_sem.at[6]).wait()
    pltpu.make_async_copy(back_slots.at[sent], back_slots.at[sent], send_sem.at[7]).wait()
    put_adv.wait()
    put_heat.wait()


def body(
    spectral,
    wavenumber_of_slot,
    filter_strength,
    courant,
    sunlit_blocks,
    sunlit_owner,
    radiation_in,
    radiation_mid,
    radiation_out,
):
    smem = pl.BlockSpec(memory_space=pltpu.SMEM)
    anywhere = pl.BlockSpec(memory_space=pl.ANY)
    dma = pltpu.SemaphoreType.DMA
    return pl.pallas_call(
        kernel,
        out_shape=(
            jax.ShapeDtypeStruct((ROWS, COLS, LEV), F32),
            jax.ShapeDtypeStruct((ROWS, COLS, LEV), BF16),
        ),
        in_specs=[smem] * 4 + [anywhere] * 6,
        out_specs=(anywhere, anywhere),
        scratch_shapes=[
            pltpu.VMEM((ROWS, 2, OWN, DEG), BF16),
            pltpu.VMEM((LAT * 16, DEG), BF16),
            pltpu.VMEM((2, ROWS, COLS, LEV), BF16),
            pltpu.VMEM((1, LEV, HID), BF16),
            pltpu.VMEM((1, HID, HID), BF16),
            pltpu.VMEM((1, HID, LEV), BF16),
            pltpu.VMEM((256, DEG), BF16),
            pltpu.VMEM((LAT, 16, LEV), BF16),
            pltpu.VMEM((LAT, 16, LEV), BF16),
            pltpu.VMEM((LAT * 16, LEV), F32),
            pltpu.VMEM((COLS, NLON), F32),
            pltpu.VMEM((LON // 2, NLON, 256), BF16),
            pltpu.VMEM((DEG, LEV), F32),
            pltpu.VMEM((LON, COLS, LEV), BF16),
            pltpu.VMEM((LON, 112, LEV), BF16),
            pltpu.VMEM((2, COLS, LEV), BF16),
            pltpu.VMEM((2, COLS, LEV), BF16),
            pltpu.VMEM((2, ROWS, 16, LEV), BF16),
            pltpu.VMEM((2, ROWS, 16, LEV), BF16),
            pltpu.VMEM((2, ROWS + 2, WIDE, LEV), F32),
            pltpu.VMEM((ROWS + 4, WIDE, LEV), F32),
            pltpu.VMEM((ROWS + 2, WIDE, LEV), F32),
            pltpu.VMEM((ROWS, COLS, LEV), F32),
            pltpu.VMEM((50, 16, LEV), BF16),
            pltpu.VMEM((2 * LON, 16, LEV), BF16),
            pltpu.VMEM((2 * LON, 16, LEV), BF16),
            pltpu.VMEM((2 * LON, 16, LEV), BF16),
            pltpu.VMEM((2 * LON + 1, 16, LEV), BF16),
            pltpu.VMEM((ROWS, COLS, LEV), BF16),
            pltpu.SMEM((32,), jnp.int32),
            pltpu.SMEM((50,), jnp.int32),
            dma((8,)),
            dma((8,)),
            dma((8,)),
        ],
        compiler_params=pltpu.CompilerParams(
            collective_id=1, has_side_effects=True, vmem_limit_bytes=48 * 1024 * 1024
        ),
        name="spectral_radiation",
    )(
        wavenumber_of_slot,
        filter_strength,
        sunlit_blocks.reshape(-1),
        sunlit_owner.reshape(-1),
        spectral,
        jnp.asarray(latitude_rows()),
        courant,
        radiation_in,
        radiation_mid,
        radiation_out,
    )


def solution(mesh):
    in_specs = (
        P("lat", None, "lon", None),
        P(),
        P("lon"),
        P(None, "lat", "lon", None),
        P("lat", "lon", None),
        P("lat", "lon", None, None),
        P("lon", None, None),
        P("lon", None, None),
        P("lon", None, None),
    )
    out_specs = (P("lat", "lon", None), P("lat", "lon", None))
    return jax.shard_map(body, mesh=mesh, in_specs=in_specs, out_specs=out_specs, check_vma=False)
```

time: 229 us -> 90.5 us (0.40)
  the two profiles are of different devices: /device:TPU:32 before, /device:TPU:1 now
where the time goes in v1:
time: 90.5 us; the launch traced here: 90.1 us
  Pallas kernels  79.3 us (88%)
  local copies, waits for them, and re-layouts  10.2 us (11%)
    pallas_call x1, Pallas kernels, body(): pl.pallas_call(kernel, out_shape=(jax.ShapeDtypeStruct((ROWS, COLS, LEV),...  79.3 us
    unnamed x22, local copies, waits for them, and re-layouts  10.2 us

profile of v1, /device:TPU:1, one launch (start us, length us, event | category | flops | bytes accessed | tf_op | source)
XLA Modules:
  0.0 90.1 jit_solution(3063052221893483123)
XLA Ops:
  0.6 0.0 copy-start
  0.6 1.3 %copy-done = bf16[1024,640]{1,0:T(8,128)(2,1)S(1)} copy-done((bf16[1024,640]{1,0:T(8,128)(2,1)S(1)}, bf16[1024,640]{1,0:T(8,128)(2,1)}, u32[]{:S(2)}) %copy-start) | copy-done | bytes 1310744
  2.0 0.0 copy-start.1
  2.0 1.0 %copy-done.1 = bf16[1,512,512]{2,1,0:T(8,128)(2,1)S(1)} copy-done((bf16[1,512,512]{2,1,0:T(8,128)(2,1)S(1)}, bf16[1,512,512]{2,1,0:T(8,128)(2,1)}, u32[]{:S(2)}) %copy-start.1) | copy-done | bytes 524312
  3.0 0.0 copy-start.2
  3.0 1.0 %copy-done.2 = bf16[2,10,80,128]{3,2,1,0:T(8,128)(2,1)S(1)} copy-done((bf16[2,10,80,128]{3,2,1,0:T(8,128)(2,1)S(1)}, bf16[2,10,80,128]{3,2,1,0:T(8,128)(2,1)}, u32[]{:S(2)}) %copy-start.2) | copy-done | bytes 409624
  4.0 0.0 copy-start.3
  4.0 0.9 %copy-done.3 = bf16[10,2,8,640]{3,2,1,0:T(8,128)(2,1)S(1)} copy-done((bf16[10,2,8,640]{3,2,1,0:T(8,128)(2,1)S(1)}, bf16[10,2,8,640]{3,2,1,0:T(8,128)(2,1)}, u32[]{:S(2)}) %copy-start.3) | copy-done | bytes 204824
  4.9 0.0 copy-start.4
  4.9 0.9 %copy-done.4 = bf16[1,128,512]{2,1,0:T(8,128)(2,1)S(1)} copy-done((bf16[1,128,512]{2,1,0:T(8,128)(2,1)S(1)}, bf16[1,128,512]{2,1,0:T(8,128)(2,1)}, u32[]{:S(2)}) %copy-start.4) | copy-done | bytes 131096
  5.8 0.0 copy-start.5
  5.8 0.9 %copy-done.5 = bf16[1,512,128]{2,1,0:T(8,128)(2,1)S(1)} copy-done((bf16[1,512,128]{2,1,0:T(8,128)(2,1)S(1)}, bf16[1,512,128]{2,1,0:T(8,128)(2,1)}, u32[]{:S(2)}) %copy-start.5) | copy-done | bytes 131096
  6.7 0.0 copy-start.6
  6.7 0.7 copy-done.6
  7.4 0.0 copy-start.7
  7.4 0.7 copy-done.7
  8.1 0.0 copy-start.8
  8.1 0.7 copy-done.8
  8.7 0.0 copy-start.9
  8.7 0.7 copy-done.9
  9.4 79.3 %spectral_radiation.1 = (f32[10,80,128]{2,1,0:T(8,128)S(1)}, bf16[10,80,128]{2,1,0:T(8,128)(2,1)S(1)}) custom-call(s32[640]{0:T(1024)S(1)} %copy-done.6, f32[8]{0:T(128)S(1)} %copy-done.7, s32[12]{0:T(128)S(1)} %bitcast.2, s32[12]{0:T(128)S(1)} %bitcast.3, bf16[10,2,8,640]{3,2,1,0:T(8,128)(2,1)S(1)} %copy-done.3, bf16[1024,640]{1,0:T(8,128)(2,1)S(1)} %copy-done, ...), custom_call_target="tpu_custom_call" | custom-call | tf_op jit(solution)/shard_map/spectral_radiation/pallas_call | solution.py:516
  88.7 0.8 copy.14
  89.4 0.7 copy.15
Async XLA Ops:
  0.6 1.3 %copy-start = (bf16[1024,640]{1,0:T(8,128)(2,1)S(1)}, bf16[1024,640]{1,0:T(8,128)(2,1)}, u32[]{:S(2)}) copy-start(bf16[1024,640]{1,0:T(8,128)(2,1)} %constant.2.clone.table_hbm) | copy-start | bytes 3932164
  2.0 1.0 %copy-start.1 = (bf16[1,512,512]{2,1,0:T(8,128)(2,1)S(1)}, bf16[1,512,512]{2,1,0:T(8,128)(2,1)}, u32[]{:S(2)}) copy-start(bf16[1,512,512]{2,1,0:T(8,128)(2,1)} %wmid_hbm.1) | copy-start | bytes 1572868
  3.0 1.0 %copy-start.2 = (bf16[2,10,80,128]{3,2,1,0:T(8,128)(2,1)S(1)}, bf16[2,10,80,128]{3,2,1,0:T(8,128)(2,1)}, u32[]{:S(2)}) copy-start(bf16[2,10,80,128]{3,2,1,0:T(8,128)(2,1)} %courant_hbm.1) | copy-start | bytes 1228804
  4.0 0.9 %copy-start.3 = (bf16[10,2,8,640]{3,2,1,0:T(8,128)(2,1)S(1)}, bf16[10,2,8,640]{3,2,1,0:T(8,128)(2,1)}, u32[]{:S(2)}) copy-start(bf16[10,2,8,640]{3,2,1,0:T(8,128)(2,1)} %spectral_hbm.1) | copy-start | bytes 614404
  4.9 0.9 %copy-start.4 = (bf16[1,128,512]{2,1,0:T(8,128)(2,1)S(1)}, bf16[1,128,512]{2,1,0:T(8,128)(2,1)}, u32[]{:S(2)}) copy-start(bf16[1,128,512]{2,1,0:T(8,128)(2,1)} %win_hbm.1) | copy-start | bytes 393220
  5.8 0.9 %copy-start.5 = (bf16[1,512,128]{2,1,0:T(8,128)(2,1)S(1)}, bf16[1,512,128]{2,1,0:T(8,128)(2,1)}, u32[]{:S(2)}) copy-start(bf16[1,512,128]{2,1,0:T(8,128)(2,1)} %wout_hbm.1) | copy-start | bytes 393220
  6.7 0.7 copy-start.6
  7.4 0.7 copy-start.7
  8.1 0.7 copy-start.8
  8.7 0.7 copy-start.9

commit v2 on v1

--- a/solution.py
+++ b/solution.py
@@ -1,4 +1,3 @@
-import functools
 import math
 
 import jax
@@ -54,15 +53,20 @@
 
 
 def silu(v):
-    return v / (1.0 + jnp.exp(-v))
-
-
-def peer_at(t, p):
-    i = t // 2
-    far = 16 - (i + 1) // 2
-    chip = lax.rem(p // 2 + jnp.where(i % 2 == 1, far, 32 - far), 32)
-    core = jnp.where(t == 62, 1 - lax.rem(p, 2), lax.rem(t, 2))
-    return jnp.where(t == 62, p // 2, chip) * 2 + core
+    half = 0.5 * v
+    return half + half * jnp.tanh(half)
+
+
+def rank_at(t, p):
+    z, k = p // 2, t // 4
+    low = jnp.minimum(z, 16)
+    down = jnp.where(k < low, low - k, k + 1)
+    first = jnp.where(z > 16, 32 - z, 1)
+    up = jnp.where(first + k < 16, first + k, 15 - k)
+    chip = lax.rem(z + jnp.where(lax.rem(t // 2, 2) == 0, 32 - down, up), 32)
+    own = t == LAT - 2
+    core = jnp.where(own, 1 - lax.rem(p, 2), lax.rem(t, 2))
+    return jnp.where(own, z, chip) * 2 + core
 
 
 def kernel(
@@ -89,10 +93,13 @@
     got,
     gotf,
     wide,
+    wide_low,
     trig,
     mcol,
     slab,
     land,
+    land_south,
+    land_north,
     c_north,
     c_south,
     c_west,
@@ -132,15 +139,14 @@
     barrier = pltpu.get_barrier_semaphore()
 
     def greet_lat(t, carry):
-        pl.semaphore_signal(barrier, inc=1, device_id=(peer_at(t, p), q), device_id_type=MESH)
+        pl.semaphore_signal(barrier, inc=1, device_id=(rank_at(t, p), q), device_id_type=MESH)
         return carry
 
     lax.fori_loop(0, LAT - 1, greet_lat, 0)
 
     def greet_lon(t, carry):
         other = lax.rem(q + t, LON)
-        for row in (p, north, south):
-            pl.semaphore_signal(barrier, inc=1, device_id=(row, other), device_id_type=MESH)
+        pl.semaphore_signal(barrier, inc=1, device_id=(p, other), device_id_type=MESH)
         return carry
 
     lax.fori_loop(1, LON, greet_lon, 0)
@@ -185,6 +191,67 @@
 
     lax.fori_loop(0, 8, over_degrees, 0)
 
+    get_cour.wait()
+    pl.semaphore_wait(barrier, LAT + LON - 2)
+
+    edge_north = pltpu.make_async_remote_copy(
+        cour.at[:, ROWS - 1],
+        c_south,
+        send_sem.at[1],
+        recv_sem.at[1],
+        device_id=(north, q),
+        device_id_type=MESH,
+    )
+    edge_south = pltpu.make_async_remote_copy(
+        cour.at[:, 0],
+        c_north,
+        send_sem.at[2],
+        recv_sem.at[2],
+        device_id=(south, q),
+        device_id_type=MESH,
+    )
+    edge_east = pltpu.make_async_remote_copy(
+        cour.at[:, :, pl.ds(COLS - 16, 16), :],
+        c_west,
+        send_sem.at[3],
+        recv_sem.at[3],
+        device_id=(p, east),
+        device_id_type=MESH,
+    )
+    edge_west = pltpu.make_async_remote_copy(
+        cour.at[:, :, pl.ds(0, 16), :],
+        c_east,
+        send_sem.at[4],
+        recv_sem.at[4],
+        device_id=(p, west),
+        device_id_type=MESH,
+    )
+    edge_east.start()
+    edge_west.start()
+
+    @pl.when(p < LAT - 1)
+    def _():
+        edge_north.start()
+
+    @pl.when(p > 0)
+    def _():
+        edge_south.start()
+
+    def send_lat(t, carry):
+        other = rank_at(t, p)
+        pltpu.make_async_remote_copy(
+            pay.at[other],
+            got.at[p],
+            send_sem.at[0],
+            recv_sem.at[0],
+            device_id=(other, q),
+            device_id_type=MESH,
+        ).start()
+        return carry
+
+    lax.fori_loop(0, LAT - 1, send_lat, 0)
+    pltpu.make_async_copy(pay.at[p], got.at[p], recv_sem.at[0]).start()
+
     sub8 = lax.broadcasted_iota(jnp.int32, (8, LEV), 0)
 
     def columns(t, carry):
@@ -207,17 +274,13 @@
         c1, d1 = circle(fraction(m * float(COLS)))
         base = pl.multiple_of(s * 128, 128)
         for other in range(LON):
-            lanes = pl.ds((other % 2) * 128, 128)
-            trig[other // 2, pl.ds(base, 64), lanes] = c.astype(BF16)
-            trig[other // 2, pl.ds(base + 64, 64), lanes] = (-d).astype(BF16)
+            lanes = pl.ds((other % 4) * 128, 128)
+            trig[other // 4, pl.ds(base, 64), lanes] = c.astype(BF16)
+            trig[other // 4, pl.ds(base + 64, 64), lanes] = (-d).astype(BF16)
             c, d = c * c1 - d * d1, d * c1 + c * d1
         return carry
 
     lax.fori_loop(0, ROWS, trig_rows, 0)
-
-    def clear_pick(t, carry):
-        pick[t] = 0
-        return carry
 
     owners = [owner_ref[t] for t in range(12)]
     listed = [sunlit_ref[t] for t in range(12)]
@@ -246,66 +309,13 @@
 
     lax.fori_loop(0, 50, fill_place, 0)
 
-    get_cour.wait()
-    pl.semaphore_wait(barrier, LAT - 1 + 3 * (LON - 1))
-
-    def send_lat(t, carry):
-        other = peer_at(t, p)
-        pltpu.make_async_remote_copy(
-            pay.at[other],
-            got.at[p],
-            send_sem.at[0],
-            recv_sem.at[0],
-            device_id=(other, q),
-            device_id_type=MESH,
-        ).start()
-        return carry
-
-    lax.fori_loop(0, LAT - 1, send_lat, 0)
-    pltpu.make_async_copy(pay.at[p], got.at[p], recv_sem.at[0]).start()
-
-    edges = [
-        pltpu.make_async_remote_copy(
-            cour.at[:, ROWS - 1],
-            c_south,
-            send_sem.at[1],
-            recv_sem.at[1],
-            device_id=(north, q),
-            device_id_type=MESH,
-        ),
-        pltpu.make_async_remote_copy(
-            cour.at[:, 0],
-            c_north,
-            send_sem.at[2],
-            recv_sem.at[2],
-            device_id=(south, q),
-            device_id_type=MESH,
-        ),
-        pltpu.make_async_remote_copy(
-            cour.at[:, :, pl.ds(COLS - 16, 16), :],
-            c_west,
-            send_sem.at[3],
-            recv_sem.at[3],
-            device_id=(p, east),
-            device_id_type=MESH,
-        ),
-        pltpu.make_async_remote_copy(
-            cour.at[:, :, pl.ds(0, 16), :],
-            c_east,
-            send_sem.at[4],
-            recv_sem.at[4],
-            device_id=(p, west),
-            device_id_type=MESH,
-        ),
-    ]
-    for edge in edges:
-        edge.start()
-    for edge in edges:
-        edge.wait()
+    edge_east.wait()
+    edge_west.wait()
     zeros8 = jnp.zeros((8, LEV), F32)
-    for k in range(2):
-        flow[k, 0] = jnp.concatenate([zeros8, c_south[k].astype(F32), zeros8], axis=0)
-        flow[k, ROWS + 1] = jnp.concatenate([zeros8, c_north[k].astype(F32), zeros8], axis=0)
+
+    def edge_row(at, edge):
+        for k in range(2):
+            flow[k, at] = jnp.concatenate([zeros8, edge[k].astype(F32), zeros8], axis=0)
 
     def fill_flow(r, carry):
         for k in range(2):
@@ -342,18 +352,20 @@
                         low, turned[at : at + 8], turned[at + 8 : at + 16]
                     )
 
+    wide_low[...] = wide[...].astype(BF16)
+
     def send_lon(t, carry):
-        pair = lax.rem(q // 2 + t, LON // 2)
-        g = jnp.dot(wide[...].astype(BF16), trig[pair], preferred_element_type=F32).astype(BF16)
-        for h in range(2):
-            other = pair * 2 + h
+        four = lax.rem(q // 4 + t, LON // 4)
+        g = jnp.dot(wide_low[...], trig[four], preferred_element_type=F32).astype(BF16)
+        for h in range(4):
+            other = four * 4 + h
             slab[other] = g[:, h * 128 : (h + 1) * 128]
 
             @pl.when(other != q)
             def _():
                 pltpu.make_async_remote_copy(
                     slab.at[other],
-                    land.at[q, pl.ds(16, 80), :],
+                    land.at[q],
                     send_sem.at[5],
                     recv_sem.at[5],
                     device_id=(p, other),
@@ -363,39 +375,69 @@
             @pl.when(other == q)
             def _():
                 pltpu.make_async_copy(
-                    slab.at[other], land.at[q, pl.ds(16, 80), :], recv_sem.at[5]
+                    slab.at[other], land.at[q], recv_sem.at[5]
                 ).start()
 
-            pltpu.make_async_remote_copy(
-                slab.at[other, pl.ds(64, 16), :],
-                land.at[q, pl.ds(0, 16), :],
-                send_sem.at[5],
-                recv_sem.at[5],
-                device_id=(north, other),
-                device_id_type=MESH,
-            ).start()
-            pltpu.make_async_remote_copy(
-                slab.at[other, pl.ds(0, 16), :],
-                land.at[q, pl.ds(96, 16), :],
-                send_sem.at[5],
-                recv_sem.at[5],
-                device_id=(south, other),
-                device_id_type=MESH,
-            ).start()
-        return carry
-
-    lax.fori_loop(0, LON // 2, send_lon, 0)
+            @pl.when(p < LAT - 1)
+            def _():
+                pltpu.make_async_remote_copy(
+                    slab.at[other, pl.ds(64, 16), :],
+                    land_south.at[q],
+                    send_sem.at[8],
+                    recv_sem.at[8],
+                    device_id=(north, other),
+                    device_id_type=MESH,
+                ).start()
+
+            @pl.when(p > 0)
+            def _():
+                pltpu.make_async_remote_copy(
+                    slab.at[other, pl.ds(0, 16), :],
+                    land_north.at[q],
+                    send_sem.at[9],
+                    recv_sem.at[9],
+                    device_id=(south, other),
+                    device_id_type=MESH,
+                ).start()
+
+        return carry
+
+    lax.fori_loop(0, LON // 4, send_lon, 0)
+    def assemble(two, at):
+        for k in range(2):
+            q_zero[at + k] = two[:, k * 8 : k * 8 + 8, :].reshape(128, 128).T[:WIDE]
+
     pltpu.make_async_copy(land, land, recv_sem.at[5]).wait()
-
-    for h in range(7):
-        two = land[:, pl.ds(h * 16, 16), :].astype(F32)
-        for k in range(2):
-            field = two[:, k * 8 : k * 8 + 8, :].reshape(128, 128).T[:WIDE]
-            if h == 0:
-                field = jnp.where(p == 0, 0.0, field)
-            if h == 6:
-                field = jnp.where(p == LAT - 1, 0.0, field)
-            q_zero[h * 2 + k] = field
+    for h in range(5):
+        assemble(land[:, pl.ds(h * 16, 16), :].astype(F32), 2 + h * 2)
+
+    @pl.when(p > 0)
+    def _():
+        pltpu.make_async_copy(land_south, land_south, recv_sem.at[8]).wait()
+        assemble(land_south[...].astype(F32), 0)
+        edge_south.wait_send()
+        edge_north.wait_recv()
+        edge_row(0, c_south)
+
+    @pl.when(p == 0)
+    def _():
+        q_zero[pl.ds(0, 2)] = jnp.zeros((2, WIDE, LEV), F32)
+        flow[0, 0] = jnp.zeros((WIDE, LEV), F32)
+        flow[1, 0] = jnp.zeros((WIDE, LEV), F32)
+
+    @pl.when(p < LAT - 1)
+    def _():
+        pltpu.make_async_copy(land_north, land_north, recv_sem.at[9]).wait()
+        assemble(land_north[...].astype(F32), ROWS + 2)
+        edge_north.wait_send()
+        edge_south.wait_recv()
+        edge_row(ROWS + 1, c_north)
+
+    @pl.when(p == LAT - 1)
+    def _():
+        q_zero[pl.ds(ROWS + 2, 2)] = jnp.zeros((2, WIDE, LEV), F32)
+        flow[0, ROWS + 1] = jnp.zeros((WIDE, LEV), F32)
+        flow[1, ROWS + 1] = jnp.zeros((WIDE, LEV), F32)
 
     def step(centre, upper, lower, u, v):
         right = pltpu.roll(centre, WIDE - 1, 0)
@@ -489,9 +531,15 @@
     pltpu.make_async_copy(pay.at[sent], pay.at[sent], send_sem.at[0]).wait()
     sent = pl.ds(0, LON - 1)
     pltpu.make_async_copy(slab.at[sent], slab.at[sent], send_sem.at[5]).wait()
-    sent = pl.ds(0, 2 * LON)
-    edge_rows = slab.at[pl.ds(0, LON), pl.ds(0, 32), :]
-    pltpu.make_async_copy(edge_rows, edge_rows, send_sem.at[5]).wait()
+
+    @pl.when(p < LAT - 1)
+    def _():
+        pltpu.make_async_copy(land_south, land_south, send_sem.at[8]).wait()
+
+    @pl.when(p > 0)
+    def _():
+        pltpu.make_async_copy(land_north, land_north, send_sem.at[9]).wait()
+
     sent = pl.ds(0, 2 * LON - 2)
     pltpu.make_async_copy(out_slots.at[sent], out_slots.at[sent], send_sem.at[6]).wait()
     pltpu.make_async_copy(back_slots.at[sent], back_slots.at[sent], send_sem.at[7]).wait()
@@ -533,10 +581,13 @@
             pltpu.VMEM((LAT, 16, LEV), BF16),
             pltpu.VMEM((LAT * 16, LEV), F32),
             pltpu.VMEM((COLS, NLON), F32),
-            pltpu.VMEM((LON // 2, NLON, 256), BF16),
+            pltpu.VMEM((COLS, NLON), BF16),
+            pltpu.VMEM((LON // 4, NLON, 512), BF16),
             pltpu.VMEM((DEG, LEV), F32),
             pltpu.VMEM((LON, COLS, LEV), BF16),
-            pltpu.VMEM((LON, 112, LEV), BF16),
+            pltpu.VMEM((LON, COLS, LEV), BF16),
+            pltpu.VMEM((LON, 16, LEV), BF16),
+            pltpu.VMEM((LON, 16, LEV), BF16),
             pltpu.VMEM((2, COLS, LEV), BF16),
             pltpu.VMEM((2, COLS, LEV), BF16),
             pltpu.VMEM((2, ROWS, 16, LEV), BF16),
@@ -554,11 +605,11 @@
             pltpu.SMEM((32,), jnp.int32),
             pltpu.SMEM((50,), jnp.int32),
             dma((8,)),
-            dma((8,)),
-            dma((8,)),
+            dma((10,)),
+            dma((10,)),
         ],
         compiler_params=pltpu.CompilerParams(
-            collective_id=1, has_side_effects=True, vmem_limit_bytes=48 * 1024 * 1024
+            collective_id=1, has_side_effects=True, vmem_limit_bytes=64 * 1024 * 1024
         ),
         name="spectral_radiation",
     )(

time: 90.5 us -> 79 us (0.87)
  the two profiles are of different devices: /device:TPU:1 before, /device:TPU:288 now
where the time goes in v2:
time: 79 us; the launch traced here: 78.8 us
  Pallas kernels  74.7 us (95%)
  local copies, waits for them, and re-layouts  3.4 us (4%)
    pallas_call x1, Pallas kernels, body(): pl.pallas_call(kernel, out_shape=(jax.ShapeDtypeStruct((ROWS, COLS, LEV),...  74.7 us
    unnamed x2, local copies, waits for them, and re-layouts  3.4 us

profile of v2, /device:TPU:288, one launch (start us, length us, event | category | flops | bytes accessed | tf_op | source)
XLA Modules:
  0.0 78.8 jit_solution(7147280819136030304)
XLA Ops:
  0.6 74.7 %spectral_radiation.1 = (f32[10,80,128]{2,1,0:T(8,128)}, bf16[10,80,128]{2,1,0:T(8,128)(2,1)}) custom-call(s32[640]{0:T(1024)} %wave_ref.1, f32[8]{0:T(128)} %strength_ref.1, s32[12]{0:T(128)} %bitcast.2, s32[12]{0:T(128)} %bitcast.3, bf16[10,2,8,640]{3,2,1,0:T(8,128)(2,1)} %spectral_hbm.1, bf16[1024,640]{1,0:T(8,128)(2,1)} %constant.2.clone.table_hbm, ...), custom_call_target="tpu_custom_call" | custom-call | tf_op jit(solution)/shard_map/spectral_radiation/pallas_call | solution.py:564
  75.4 1.8 %copy.14 = f32[10,80,128]{2,1,0:T(8,128)} copy(f32[10,80,128]{2,1,0:T(8,128)} %get-tuple-element.4) | data formatting | bytes 819200
  77.1 1.6 %copy.15 = bf16[10,80,128]{2,1,0:T(8,128)(2,1)} copy(bf16[10,80,128]{2,1,0:T(8,128)(2,1)} %get-tuple-element.5) | data formatting | bytes 409600

commit v3 on v2

--- a/solution.py
+++ b/solution.py
@@ -1,3 +1,4 @@
+import functools
 import math
 
 import jax
@@ -23,6 +24,7 @@
 LEAD = 8
 WIDE = 96
 HID = 512
+PACK = 14
 
 
 def latitude_rows():
@@ -57,16 +59,28 @@
     return half + half * jnp.tanh(half)
 
 
-def rank_at(t, p):
+REACH = 8
+NEAR = 4 * REACH + 1
+FAR = LAT - 1 - NEAR
+
+
+def rank_at(t, p, least, down_most, up_most):
     z, k = p // 2, t // 4
-    low = jnp.minimum(z, 16)
-    down = jnp.where(k < low, low - k, k + 1)
-    first = jnp.where(z > 16, 32 - z, 1)
-    up = jnp.where(first + k < 16, first + k, 15 - k)
+    low = jnp.minimum(z, down_most)
+    down = jnp.where(k < low - least + 1, low - k, least + k)
+    first = jnp.where(z > 31 - up_most, jnp.maximum(32 - z, least), least)
+    up = jnp.where(first + k <= up_most, first + k, up_most - k)
     chip = lax.rem(z + jnp.where(lax.rem(t // 2, 2) == 0, 32 - down, up), 32)
-    own = t == LAT - 2
-    core = jnp.where(own, 1 - lax.rem(p, 2), lax.rem(t, 2))
-    return jnp.where(own, z, chip) * 2 + core
+    return chip * 2 + lax.rem(t, 2)
+
+
+def near_rank(t, p):
+    other = rank_at(t, p, 1, REACH, REACH)
+    return jnp.where(t == NEAR - 1, p + 1 - 2 * lax.rem(p, 2), other)
+
+
+def far_rank(t, p):
+    return rank_at(t, p, REACH + 1, 16, 15)
 
 
 def kernel(
@@ -119,6 +133,7 @@
     local_sem,
     send_sem,
     recv_sem,
+    heard,
 ):
     p = lax.axis_index("lat")
     q = lax.axis_index("lon")
@@ -139,10 +154,10 @@
     barrier = pltpu.get_barrier_semaphore()
 
     def greet_lat(t, carry):
-        pl.semaphore_signal(barrier, inc=1, device_id=(rank_at(t, p), q), device_id_type=MESH)
-        return carry
-
-    lax.fori_loop(0, LAT - 1, greet_lat, 0)
+        pl.semaphore_signal(barrier, inc=1, device_id=(near_rank(t, p), q), device_id_type=MESH)
+        return carry
+
+    lax.fori_loop(0, NEAR, greet_lat, 0)
 
     def greet_lon(t, carry):
         other = lax.rem(q + t, LON)
@@ -174,25 +189,28 @@
         damp[pl.ds(s * 16, 16), :] = both
         if s >= 8:
             damp[pl.ds(s * 16 + 32, 16), :] = both
-    damp[pl.ds(192, 64), :] = jnp.zeros((64, DEG), BF16)
+            damp[pl.ds(s * 16 + 64, 16), :] = both
+    damp[pl.ds(224, 32), :] = jnp.zeros((32, DEG), BF16)
 
     get_table.wait()
-    row16 = lax.broadcasted_iota(jnp.int32, (128, LEV), 0) % 16
-    lane = lax.broadcasted_iota(jnp.int32, (128, LEV), 1)
-
-    def over_degrees(t, carry):
-        rows = table[pl.ds(pl.multiple_of(t * 128, 128), 128), :]
-        y = lax.dot_general(rows, damp[...], (((1,), (1,)), ((), ())), preferred_element_type=F32)
-        first, last = y[:, :128], y[:, 128:]
-        tail = jnp.where(lane < 32, last, pltpu.roll(last, 6, 0))
-        packed = jnp.where(row16 < ROWS, first, tail).astype(BF16)
-        pay[pl.ds(t * 8, 8)] = packed.reshape(8, 16, LEV)
-        return carry
-
-    lax.fori_loop(0, 8, over_degrees, 0)
+    row16 = lax.broadcasted_iota(jnp.int32, (LAT * 16, LEV), 0) % 16
+    lane = lax.broadcasted_iota(jnp.int32, (LAT * 16, LEV), 1)
+    y = lax.dot_general(
+        table[...], damp[...], (((1,), (1,)), ((), ())), preferred_element_type=F32
+    )
+    first, last = y[:, :128], y[:, 128:]
+    tail = jnp.where(
+        lane < 32, last, jnp.where(lane < 64, pltpu.roll(last, 6, 0), pltpu.roll(last, 2, 0))
+    )
+    packed = jnp.where(row16 < ROWS, first, tail).astype(BF16)
+    pay[...] = packed.reshape(LAT, 8, 2, LEV)[:, : PACK // 2]
 
     get_cour.wait()
-    pl.semaphore_wait(barrier, LAT + LON - 2)
+    pl.semaphore_wait(barrier, NEAR + LON - 1)
+    for d in (REACH, 32 - REACH):
+        pl.semaphore_signal(
+            heard, inc=1, device_id=(lax.rem(p + 2 * d, LAT), q), device_id_type=MESH
+        )
 
     edge_north = pltpu.make_async_remote_copy(
         cour.at[:, ROWS - 1],
@@ -226,19 +244,8 @@
         device_id=(p, west),
         device_id_type=MESH,
     )
-    edge_east.start()
-    edge_west.start()
-
-    @pl.when(p < LAT - 1)
-    def _():
-        edge_north.start()
-
-    @pl.when(p > 0)
-    def _():
-        edge_south.start()
-
-    def send_lat(t, carry):
-        other = rank_at(t, p)
+    def send_lat(rank_of, t, carry):
+        other = rank_of(t, p)
         pltpu.make_async_remote_copy(
             pay.at[other],
             got.at[p],
@@ -249,8 +256,11 @@
         ).start()
         return carry
 
-    lax.fori_loop(0, LAT - 1, send_lat, 0)
+    lax.fori_loop(0, NEAR, functools.partial(send_lat, near_rank), 0)
     pltpu.make_async_copy(pay.at[p], got.at[p], recv_sem.at[0]).start()
+
+    edge_east.start()
+    edge_west.start()
 
     sub8 = lax.broadcasted_iota(jnp.int32, (8, LEV), 0)
 
@@ -282,6 +292,16 @@
 
     lax.fori_loop(0, ROWS, trig_rows, 0)
 
+    pl.semaphore_wait(heard, 2)
+    lax.fori_loop(0, FAR, functools.partial(send_lat, far_rank), 0)
+    @pl.when(p < LAT - 1)
+    def _():
+        edge_north.start()
+
+    @pl.when(p > 0)
+    def _():
+        edge_south.start()
+
     owners = [owner_ref[t] for t in range(12)]
     listed = [sunlit_ref[t] for t in range(12)]
     slots = []
@@ -332,10 +352,10 @@
     lax.fori_loop(0, ROWS, fill_flow, 0)
 
     pltpu.make_async_copy(got, got, recv_sem.at[0]).wait()
-    gotf[...] = got[...].astype(F32).reshape(LAT * 16, LEV)
+    gotf[...] = got[...].astype(F32).reshape(LAT * PACK, LEV)
     low = lax.broadcasted_iota(jnp.int32, (8, LEV), 1) < 64
-    for r in range(16):
-        part = gotf[pl.ds(r, LAT, stride=16), :]
+    for r in range(PACK):
+        part = gotf[pl.ds(r, LAT, stride=PACK), :]
         turned = jnp.concatenate([part, part], axis=0).T
         if r < ROWS:
             for a in range(8):
@@ -343,9 +363,7 @@
                     low, turned[a * 16 : a * 16 + 8], turned[a * 16 + 8 : a * 16 + 16]
                 )
         else:
-            for g, jj in ((0, r - ROWS), (1, r - ROWS + 4)):
-                if g == 1 and jj < 6:
-                    continue
+            for g, jj in enumerate(range(r - ROWS, ROWS, 4)):
                 for a in range(2):
                     at = g * 32 + a * 16
                     wide[pl.ds(jj * 8, 8), pl.ds((8 + a) * 128, 128)] = jnp.where(
@@ -466,14 +484,13 @@
     put_adv = pltpu.make_async_copy(adv, advected_hbm, local_sem.at[6])
     put_adv.start()
 
-    def pack(k, carry):
-        out_slots[k] = state[pick[k]]
-        return carry
-
-    lax.fori_loop(0, 2 * LON, pack, 0)
+    def pack(other):
+        for k in range(2):
+            out_slots[other * 2 + k] = state[pick[other * 2 + k]]
 
     def send_out(t, carry):
         other = lax.rem(q + t, LON)
+        pack(other)
         pltpu.make_async_remote_copy(
             out_slots.at[pl.ds(other * 2, 2)],
             in_slots.at[pl.ds(q * 2, 2)],
@@ -485,6 +502,7 @@
         return carry
 
     lax.fori_loop(1, LON, send_out, 0)
+    pack(q)
     pltpu.make_async_copy(
         out_slots.at[pl.ds(q * 2, 2)], in_slots.at[pl.ds(q * 2, 2)], recv_sem.at[6]
     ).start()
@@ -577,9 +595,9 @@
             pltpu.VMEM((1, HID, HID), BF16),
             pltpu.VMEM((1, HID, LEV), BF16),
             pltpu.VMEM((256, DEG), BF16),
-            pltpu.VMEM((LAT, 16, LEV), BF16),
-            pltpu.VMEM((LAT, 16, LEV), BF16),
-            pltpu.VMEM((LAT * 16, LEV), F32),
+            pltpu.VMEM((LAT, PACK // 2, 2, LEV), BF16),
+            pltpu.VMEM((LAT, PACK // 2, 2, LEV), BF16),
+            pltpu.VMEM((LAT * PACK, LEV), F32),
             pltpu.VMEM((COLS, NLON), F32),
             pltpu.VMEM((COLS, NLON), BF16),
             pltpu.VMEM((LON // 4, NLON, 512), BF16),
@@ -607,6 +625,7 @@
             dma((8,)),
             dma((10,)),
             dma((10,)),
+            pltpu.SemaphoreType.REGULAR,
         ],
         compiler_params=pltpu.CompilerParams(
             collective_id=1, has_side_effects=True, vmem_limit_bytes=64 * 1024 * 1024

time: 79 us -> 76.8 us (0.972)
  the two profiles are of different devices: /device:TPU:288 before, /device:TPU:32 now
where the time goes in v3:
time: 76.8 us; the launch traced here: 76.5 us
  Pallas kernels  72.5 us (94%)
  local copies, waits for them, and re-layouts  3.4 us (4%)
    pallas_call x1, Pallas kernels, body(): pl.pallas_call(kernel, out_shape=(jax.ShapeDtypeStruct((ROWS, COLS, LEV),...  72.5 us
    unnamed x2, local copies, waits for them, and re-layouts  3.4 us

profile of v3, /device:TPU:32, one launch (start us, length us, event | category | flops | bytes accessed | tf_op | source)
XLA Modules:
  0.0 76.5 jit_solution(8166234026484474056)
XLA Ops:
  0.6 72.5 %spectral_radiation.1 = (f32[10,80,128]{2,1,0:T(8,128)}, bf16[10,80,128]{2,1,0:T(8,128)(2,1)}) custom-call(s32[640]{0:T(1024)} %wave_ref.1, f32[8]{0:T(128)} %strength_ref.1, s32[12]{0:T(128)} %bitcast.2, s32[12]{0:T(128)} %bitcast.3, bf16[10,2,8,640]{3,2,1,0:T(8,128)(2,1)} %spectral_hbm.1, bf16[1024,640]{1,0:T(8,128)(2,1)} %constant.2.clone.table_hbm, ...), custom_call_target="tpu_custom_call" | custom-call | tf_op jit(solution)/shard_map/spectral_radiation/pallas_call | solution.py:582
  73.1 1.8 %copy.14 = f32[10,80,128]{2,1,0:T(8,128)} copy(f32[10,80,128]{2,1,0:T(8,128)} %get-tuple-element.4) | data formatting | bytes 819200
  74.9 1.6 %copy.15 = bf16[10,80,128]{2,1,0:T(8,128)(2,1)} copy(bf16[10,80,128]{2,1,0:T(8,128)(2,1)} %get-tuple-element.5) | data formatting | bytes 409600

commit v4 on v3

--- a/solution.py
+++ b/solution.py
@@ -565,6 +565,29 @@
     put_heat.wait()
 
 
+def hand_out(advected_hbm, heating_hbm, advected_out, heating_out, adv, heat, in_sem, out_sem):
+    ways = []
+    for k in range(2):
+        part = pl.ds(k * (ROWS // 2), ROWS // 2)
+        for source, held, target, at in (
+            (advected_hbm, adv, advected_out, k),
+            (heating_hbm, heat, heating_out, 2 + k),
+        ):
+            ways.append(
+                (
+                    pltpu.make_async_copy(source.at[part], held.at[part], in_sem.at[at]),
+                    pltpu.make_async_copy(held.at[part], target.at[part], out_sem.at[at]),
+                )
+            )
+    for there, _ in ways:
+        there.start()
+    for there, back in ways:
+        there.wait()
+        back.start()
+    for _, back in ways:
+        back.wait()
+
+
 def body(
     spectral,
     wavenumber_of_slot,
@@ -579,12 +602,13 @@
     smem = pl.BlockSpec(memory_space=pltpu.SMEM)
     anywhere = pl.BlockSpec(memory_space=pl.ANY)
     dma = pltpu.SemaphoreType.DMA
-    return pl.pallas_call(
+    outs = (
+        jax.ShapeDtypeStruct((ROWS, COLS, LEV), F32),
+        jax.ShapeDtypeStruct((ROWS, COLS, LEV), BF16),
+    )
+    advected, heating = pl.pallas_call(
         kernel,
-        out_shape=(
-            jax.ShapeDtypeStruct((ROWS, COLS, LEV), F32),
-            jax.ShapeDtypeStruct((ROWS, COLS, LEV), BF16),
-        ),
+        out_shape=outs,
         in_specs=[smem] * 4 + [anywhere] * 6,
         out_specs=(anywhere, anywhere),
         scratch_shapes=[
@@ -643,6 +667,20 @@
         radiation_mid,
         radiation_out,
     )
+    return pl.pallas_call(
+        hand_out,
+        out_shape=outs,
+        in_specs=[anywhere] * 2,
+        out_specs=(anywhere, anywhere),
+        scratch_shapes=[
+            pltpu.VMEM((ROWS, COLS, LEV), F32),
+            pltpu.VMEM((ROWS, COLS, LEV), BF16),
+            dma((4,)),
+            dma((4,)),
+        ],
+        name="hand_out",
+        compiler_params=pltpu.CompilerParams(vmem_limit_bytes=64 * 1024 * 1024),
+    )(advected, heating)
 
 
 def solution(mesh):

time: 76.8 us -> 75.2 us (0.979)
  local copies, waits for them, and re-layouts: 3.4 us -> 0 us
  Pallas kernels: 72.5 us -> 74.4 us
    unnamed x2 -> x0, local copies, waits for them, and re-layouts: 3.4 us -> none
    pallas_call x1 -> x2, Pallas kernels: 72.5 us -> 74.4 us  [the longest x1 72.5 us: body(): pl.pallas_call(kernel, out_shape=outs, in_specs=[smem] * 4 + [anywhere] *...]
where the time goes in v4:
time: 75.2 us; the launch traced here: 75 us
  Pallas kernels  74.4 us (99%)
    pallas_call x1, Pallas kernels, body(): pl.pallas_call(kernel, out_shape=outs, in_specs=[smem] * 4 + [anywhere] *...  72.5 us
    pallas_call x1, Pallas kernels, body(): pl.pallas_call(hand_out, out_shape=outs, in_specs=[anywhere] * 2, out_spe...  1.86 us

profile of v4, /device:TPU:32, one launch (start us, length us, event | category | flops | bytes accessed | tf_op | source)
XLA Modules:
  0.0 75.0 jit_solution(10495392793070722601)
XLA Ops:
  0.6 72.5 %spectral_radiation.1 = (f32[10,80,128]{2,1,0:T(8,128)}, bf16[10,80,128]{2,1,0:T(8,128)(2,1)}) custom-call(s32[640]{0:T(1024)} %wave_ref.1, f32[8]{0:T(128)} %strength_ref.1, s32[12]{0:T(128)} %bitcast.2, s32[12]{0:T(128)} %bitcast.3, bf16[10,2,8,640]{3,2,1,0:T(8,128)(2,1)} %spectral_hbm.1, bf16[1024,640]{1,0:T(8,128)(2,1)} %constant.2.clone.table_hbm, ...), custom_call_target="tpu_custom_call" | custom-call | tf_op jit(solution)/shard_map/spectral_radiation/pallas_call | solution.py:609
  73.1 1.9 %hand_out.1 = (f32[10,80,128]{2,1,0:T(8,128)}, bf16[10,80,128]{2,1,0:T(8,128)(2,1)}) custom-call(f32[10,80,128]{2,1,0:T(8,128)} %get-tuple-element.4.advected_hbm, bf16[10,80,128]{2,1,0:T(8,128)(2,1)} %get-tuple-element.5.heating_hbm), custom_call_target="tpu_custom_call" | custom-call | tf_op jit(solution)/shard_map/hand_out/pallas_call | solution.py:670

commit v5 on v4

--- a/solution.py
+++ b/solution.py
@@ -262,6 +262,16 @@
     edge_east.start()
     edge_west.start()
 
+    pl.semaphore_wait(heard, 2)
+    lax.fori_loop(0, FAR, functools.partial(send_lat, far_rank), 0)
+    @pl.when(p < LAT - 1)
+    def _():
+        edge_north.start()
+
+    @pl.when(p > 0)
+    def _():
+        edge_south.start()
+
     sub8 = lax.broadcasted_iota(jnp.int32, (8, LEV), 0)
 
     def columns(t, carry):
@@ -291,16 +301,6 @@
         return carry
 
     lax.fori_loop(0, ROWS, trig_rows, 0)
-
-    pl.semaphore_wait(heard, 2)
-    lax.fori_loop(0, FAR, functools.partial(send_lat, far_rank), 0)
-    @pl.when(p < LAT - 1)
-    def _():
-        edge_north.start()
-
-    @pl.when(p > 0)
-    def _():
-        edge_south.start()
 
     owners = [owner_ref[t] for t in range(12)]
     listed = [sunlit_ref[t] for t in range(12)]

time: 75.2 us -> 74.9 us (level)
  no operation moved by 1% of the time
where the time goes in v5:
time: 74.9 us; the launch traced here: 74.7 us
  Pallas kernels  74.1 us (99%)
    pallas_call x1, Pallas kernels, body(): pl.pallas_call(kernel, out_shape=outs, in_specs=[smem] * 4 + [anywhere] *...  72.2 us
    pallas_call x1, Pallas kernels, body(): pl.pallas_call(hand_out, out_shape=outs, in_specs=[anywhere] * 2, out_spe...  1.86 us

profile of v5, /device:TPU:32, one launch (start us, length us, event | category | flops | bytes accessed | tf_op | source)
XLA Modules:
  0.0 74.7 jit_solution(7481586970167975152)
XLA Ops:
  0.6 72.2 %spectral_radiation.1 = (f32[10,80,128]{2,1,0:T(8,128)}, bf16[10,80,128]{2,1,0:T(8,128)(2,1)}) custom-call(s32[640]{0:T(1024)} %wave_ref.1, f32[8]{0:T(128)} %strength_ref.1, s32[12]{0:T(128)} %bitcast.2, s32[12]{0:T(128)} %bitcast.3, bf16[10,2,8,640]{3,2,1,0:T(8,128)(2,1)} %spectral_hbm.1, bf16[1024,640]{1,0:T(8,128)(2,1)} %constant.2.clone.table_hbm, ...), custom_call_target="tpu_custom_call" | custom-call | tf_op jit(solution)/shard_map/spectral_radiation/pallas_call | solution.py:609
  72.8 1.9 %hand_out.1 = (f32[10,80,128]{2,1,0:T(8,128)}, bf16[10,80,128]{2,1,0:T(8,128)(2,1)}) custom-call(f32[10,80,128]{2,1,0:T(8,128)} %get-tuple-element.4.advected_hbm, bf16[10,80,128]{2,1,0:T(8,128)(2,1)} %get-tuple-element.5.heating_hbm), custom_call_target="tpu_custom_call" | custom-call | tf_op jit(solution)/shard_map/hand_out/pallas_call | solution.py:670
